TPU v7x, 128 devices: a whole 4x4x4 slice. The times are simulated.
128 devices in a mesh: row: 8 (over x_lo, y), col: 16 (over x_hi, z, core).
Axes of the slice: x: 4 (x_hi: 2, x_lo: 2; x = x_hi * 2 + x_lo), y: 4, z: 4, core: 2. Of those that a mesh axis runs over, the one named last changes fastest.
Arguments:
- inverse: bfloat16 [26624, 26624], P('row', 'col'), may hold values from -6 to 6
- panels: bfloat16 [2, 8192, 512], P(None, 'col'), may hold values from -0.0625 to 0.0625
- block_slot: int32 [208], replicated, may hold values from 0 to 207, as said below
- list_ids: int32 [2, 64], replicated, may hold values from 0 to 207, as said below
Outputs:
- packed_panels: float32 [2, 16384, 512], P(None, ('row', 'col'))
- diag_update: float32 [2, 512, 512], replicated
Inputs may be any that keep to these rules, and one draw needn't show every extreme that they name: block_slot is a permutation of the slots. `list_ids`: each supernode lists distinct blocks; at most 16 of a supernode's listed blocks have slots in one grid row (slot // 26 equal), and in every supernode some grid row holds exactly 16. `list_ids`: in each aligned group of 4 list positions of a supernode, at most 1 listed blocks have slots in one grid column (slot // 13 equal).
All inputs are finite; a program needn't handle non-finite values.
Results may differ from a plain program's by a relative error of at most 0.0003.
Values may be sent and summed in bfloat16 or wider, within the bound.
A program may use at most 128 MiB of HBM per device.

v0:
```python
import jax
import jax.numpy as jnp
from jax import lax
from jax.sharding import PartitionSpec as P

BS = 128


def split_up(array, dim, devices):
    dims = array.shape
    pieces = array.reshape(*dims[:dim], devices, dims[dim] // devices, *dims[dim + 1 :])
    return jnp.moveaxis(pieces, dim, 0)


def sent_and_summed(array, axis, dim):
    pieces = split_up(array, dim, lax.axis_size(axis))
    arrived = lax.all_to_all(pieces, axis, split_axis=0, concat_axis=0, tiled=True)
    return arrived.astype(jnp.float32).sum(axis=0)


def lookup_slots(block_slot, list_ids):
    block_ids = jnp.arange(block_slot.shape[0], dtype=jnp.int32)
    matches = list_ids[..., None] == block_ids
    return jnp.sum(jnp.where(matches, block_slot, 0), axis=-1)


def exact_product(left_rows, right_rows):
    return jnp.dot(left_rows.astype(jnp.float32).T, right_rows, precision=lax.Precision.HIGHEST)


def local(inverse, panels, block_slot, list_ids):
    panel_width = panels.shape[2]
    row_blocks = inverse.shape[0] // BS
    col_blocks = inverse.shape[1] // BS
    listed = list_ids.shape[1]
    grid_rows = lax.axis_size("row")
    grid_cols = lax.axis_size("col")
    max_rows = 2 * listed // grid_rows
    own_rows = max_rows * BS // grid_cols
    shard_len = panels.shape[1] // BS
    slot_cap = (col_blocks + grid_cols - 1) // grid_cols
    my_row = lax.axis_index("row")
    my_col = lax.axis_index("col")
    slots = lookup_slots(block_slot, list_ids)
    grid_row = slots // row_blocks
    local_row = slots % row_blocks
    grid_col = slots // col_blocks
    local_col = slots % col_blocks
    a_blocks = inverse.reshape(row_blocks, BS, col_blocks * BS)
    positions = jnp.arange(listed, dtype=jnp.int32)
    col_ids = jnp.arange(col_blocks, dtype=jnp.int32)
    shard_of = positions // shard_len
    local_pos = my_col * shard_len + jnp.arange(shard_len, dtype=jnp.int32)
    panel_sums = []
    diag_terms = []
    for supernode in range(panels.shape[0]):
        cols_here = grid_col[supernode]
        in_row = grid_row[supernode] == my_row
        chosen_pos = jnp.argsort(jnp.where(in_row, positions, listed + positions), stable=True)[
            :max_rows
        ]
        is_valid = in_row[chosen_pos]
        picked = a_blocks[local_row[supernode][chosen_pos]]
        picked = jnp.where(is_valid[:, None, None], picked, jnp.zeros((), jnp.bfloat16)).reshape(
            max_rows * BS, col_blocks * BS
        )
        local_blocks = panels[supernode].reshape(shard_len, BS, panel_width)
        same_group = (
            (cols_here[:, None] == cols_here[None, :])
            & (shard_of[:, None] == shard_of[None, :])
            & (positions[None, :] < positions[:, None])
        )
        same_rank = jnp.sum(same_group.astype(jnp.int32), axis=1)
        dest_ids = jnp.arange(grid_cols * slot_cap, dtype=jnp.int32)
        send_pick = (
            (cols_here[local_pos] * slot_cap + same_rank[local_pos])[None, :] == dest_ids[:, None]
        ).astype(jnp.bfloat16)
        outgoing = jnp.einsum(
            "mj,jbw->mbw", send_pick, local_blocks, preferred_element_type=jnp.float32
        )
        outgoing = outgoing.astype(jnp.bfloat16).reshape(grid_cols * slot_cap * BS, panel_width)
        incoming = lax.all_to_all(outgoing, "col", split_axis=0, concat_axis=0, tiled=True)
        incoming = incoming.reshape(grid_cols * slot_cap, BS, panel_width)
        mine_here = cols_here == my_col
        to_column = (
            mine_here[:, None] & (local_col[supernode][:, None] == col_ids[None, :])
        ).astype(jnp.float32)
        to_slot = ((shard_of * slot_cap + same_rank)[:, None] == dest_ids[None, :]).astype(
            jnp.float32
        )
        select = jnp.dot(to_column.T, to_slot).astype(jnp.bfloat16)
        chosen = jnp.einsum("kj,jbw->kbw", select, incoming, preferred_element_type=jnp.float32)
        chosen = chosen.astype(jnp.bfloat16).reshape(col_blocks * BS, panel_width)
        place = ((chosen_pos[:, None] == local_pos[None, :]) & is_valid[:, None]).astype(
            jnp.bfloat16
        )
        left_local = jnp.einsum(
            "kj,jbw->kbw", place, local_blocks, preferred_element_type=jnp.float32
        )
        left_local = left_local.reshape(max_rows * BS, panel_width)

        def partial_rows(first_row, row_count, picked=picked, chosen=chosen):
            return jnp.dot(picked, chosen, preferred_element_type=jnp.float32)

        mine_sums = lax.psum_scatter(
            partial_rows(jnp.int32(0), own_rows * lax.axis_size("col")),
            "col",
            scatter_dimension=0,
            tiled=True,
        )
        own_left = sent_and_summed(left_local.astype(jnp.bfloat16), "col", 0).astype(jnp.bfloat16)
        contrib = exact_product(own_left, mine_sums)
        panel_sums.append(mine_sums)
        diag_terms.append(contrib)
    diag_total = lax.psum(jnp.stack(diag_terms), ("row", "col"))
    return (jnp.stack(panel_sums), -diag_total)


def solution(mesh):
    return jax.shard_map(
        local,
        mesh=mesh,
        in_specs=(P("row", "col"), P(None, "col", None), P(), P()),
        out_specs=(P(None, ("row", "col"), None), P()),
        check_vma=False,
    )
```

profile of v0, /device:TPU:1, one launch (start us, length us, event | category | flops | bytes accessed | tf_op | source)
XLA Modules:
  0.0 414.8 jit_solution(4478664436259446148)
XLA Ops:
  7.2 0.9 select_reduce_fusion
  8.1 1.3 fusion.60
  9.4 0.6 gather_fusion.8
  10.2 0.6 gather_fusion.9
  10.9 0.9 convolution_convert_fusion.2
  11.7 2.5 copy.41
  14.2 9.3 %all-to-all-start.1 = ((bf16[16,128,512]{2,1,0:T(8,128)(2,1)}), bf16[16,128,512]{2,1,0:T(8,128)(2,1)S(1)}, u32[]{:S(2)}, u32[]{:S(2)}) async-start(bf16[16,128,512]{2,1,0:T(8,128)(2,1)} %copy.41), calls=%async_computation.2 | async-start | bytes 4194304 | tf_op jit(solution)/shard_map/all_to_all | solution.py:82
  23.6 2.0 sort.32
  25.6 0.7 gather_fusion.6
  26.3 0.7 gather_fusion.5
  27.0 8.2 %gather_fusion.7 = bf16[16,128,1664]{2,1,0:T(8,128)(2,1)} fusion(bf16[26,128,1664]{2,1,0:T(8,128)(2,1)} %bitcast.73, s32[1024]{0:T(1024)S(1)} %pad_clamp_fusion), kind=kCustom, calls=%fused_computation.7 | custom fusion | bytes 13631552 | tf_op jit(solution)/shard_map/gather | solution.py:63
  35.2 6.4 %broadcast_select_fusion = bf16[16,128,1664]{2,1,0:T(8,128)(2,1)} fusion(bf16[16,128,1664]{2,1,0:T(8,128)(2,1)} %gather_fusion.7, pred[16]{0:T(512)(128)(4,1)S(1)} %gather_fusion.5), kind=kLoop, calls=%fused_computation.10 | loop fusion | flops 3407872 | bytes 13631504 | tf_op jit(solution)/shard_map/jit(_where)/select_n | solution.py:64
  41.6 10.4 %all-to-all-done.1 = bf16[16,128,512]{2,1,0:T(8,128)(2,1)S(1)} async-done(((bf16[16,128,512]{2,1,0:T(8,128)(2,1)}), bf16[16,128,512]{2,1,0:T(8,128)(2,1)S(1)}, u32[]{:S(2)}, u32[]{:S(2)}) %all-to-all-start.1) | async-done | bytes 2097184 | tf_op jit(solution)/shard_map/all_to_all | solution.py:82
  52.0 2.8 fusion.7
  54.8 2.6 copy.43
  57.4 8.6 %fusion.64 = f32[2048,512]{1,0:T(8,128)} fusion(bf16[2048,1664]{1,0:T(8,128)(2,1)} %bitcast.76, bf16[1664,512]{1,0:T(8,128)(2,1)S(1)} %bitcast.81), kind=kOutput, calls=%fused_computation.117 | convolution fusion | flops 3489660928 | bytes 12713984 | tf_op jit(solution)/shard_map/dot_general | solution.py:103
  66.0 0.6 gather_fusion.3
  66.7 0.6 gather_fusion.4
  67.3 0.9 convolution_convert_fusion.3
  68.2 2.5 copy.37
  70.7 7.1 %all-to-all-start = ((bf16[16,128,512]{2,1,0:T(8,128)(2,1)}), bf16[16,128,512]{2,1,0:T(8,128)(2,1)S(1)}, u32[]{:S(2)}, u32[]{:S(2)}) async-start(bf16[16,128,512]{2,1,0:T(8,128)(2,1)} %copy.37), calls=%async_computation | async-start | bytes 4194304 | tf_op jit(solution)/shard_map/all_to_all | solution.py:82
  78.0 2.0 sort.31
  80.1 0.7 gather_fusion.1
  80.8 8.8 %gather_fusion.2 = bf16[16,128,1664]{2,1,0:T(8,128)(2,1)} fusion(bf16[26,128,1664]{2,1,0:T(8,128)(2,1)} %bitcast.74, s32[1024]{0:T(1024)S(1)} %pad_clamp_fusion.3), kind=kCustom, calls=%fused_computation.2 | custom fusion | bytes 13631552 | tf_op jit(solution)/shard_map/gather | solution.py:63
  89.5 0.7 gather_fusion
  90.2 6.4 %broadcast_select_fusion.1 = bf16[16,128,1664]{2,1,0:T(8,128)(2,1)} fusion(bf16[16,128,1664]{2,1,0:T(8,128)(2,1)} %gather_fusion.2, pred[16]{0:T(512)(128)(4,1)S(1)} %gather_fusion), kind=kLoop, calls=%fused_computation.11 | loop fusion | flops 3407872 | bytes 13631504 | tf_op jit(solution)/shard_map/jit(_where)/select_n | solution.py:64
  96.6 9.7 %all-to-all-done = bf16[16,128,512]{2,1,0:T(8,128)(2,1)S(1)} async-done(((bf16[16,128,512]{2,1,0:T(8,128)(2,1)}), bf16[16,128,512]{2,1,0:T(8,128)(2,1)S(1)}, u32[]{:S(2)}, u32[]{:S(2)}) %all-to-all-start) | async-done | bytes 2097184 | tf_op jit(solution)/shard_map/all_to_all | solution.py:82
  106.3 2.8 fusion.4
  109.1 2.6 copy.39
  111.7 8.5 %fusion.63 = f32[2048,512]{1,0:T(8,128)} fusion(bf16[2048,1664]{1,0:T(8,128)(2,1)} %bitcast.75, bf16[1664,512]{1,0:T(8,128)(2,1)S(1)} %bitcast.82), kind=kOutput, calls=%fused_computation.116 | convolution fusion | flops 3489660928 | bytes 12713984 | tf_op jit(solution)/shard_map/dot_general | solution.py:103
  120.3 0.9 convolution_convert_fusion
  121.2 2.5 copy.47
  123.7 10.4 %all-to-all-start.3 = ((bf16[16,128,512]{2,1,0:T(8,128)(2,1)}), bf16[16,128,512]{2,1,0:T(8,128)(2,1)S(1)}, u32[]{:S(2)}, u32[]{:S(2)}) async-start(bf16[16,128,512]{2,1,0:T(8,128)(2,1)} %copy.47), calls=%async_computation.5 | async-start | bytes 4194304 | tf_op jit(solution)/shard_map/all_to_all | solution.py:17
  134.0 0.9 convolution_convert_fusion.1
  134.9 2.5 copy.45
  137.3 28.3 %all-to-all-done.3 = bf16[16,128,512]{2,1,0:T(8,128)(2,1)S(1)} async-done(((bf16[16,128,512]{2,1,0:T(8,128)(2,1)}), bf16[16,128,512]{2,1,0:T(8,128)(2,1)S(1)}, u32[]{:S(2)}, u32[]{:S(2)}) %all-to-all-start.3) | async-done | bytes 2097184 | tf_op jit(solution)/shard_map/all_to_all | solution.py:17
  165.7 7.6 %all-to-all-start.2 = ((bf16[16,128,512]{2,1,0:T(8,128)(2,1)}), bf16[16,128,512]{2,1,0:T(8,128)(2,1)}, u32[]{:S(2)}, u32[]{:S(2)}) async-start(bf16[16,128,512]{2,1,0:T(8,128)(2,1)} %copy.45), calls=%async_computation.4 | async-start | bytes 4194304 | tf_op jit(solution)/shard_map/all_to_all | solution.py:17
  173.5 0.3 reduce_sum.55
  173.8 28.0 %all-to-all-done.2 = bf16[16,128,512]{2,1,0:T(8,128)(2,1)} async-done(((bf16[16,128,512]{2,1,0:T(8,128)(2,1)}), bf16[16,128,512]{2,1,0:T(8,128)(2,1)}, u32[]{:S(2)}, u32[]{:S(2)}) %all-to-all-start.2) | async-done | bytes 2097184 | tf_op jit(solution)/shard_map/all_to_all | solution.py:17
  201.8 1.9 reduce_sum.54
  203.8 1.6 convolution_bitcast_fusion
  205.4 43.9 %reduce-scatter.3.cloned.1.call-done = f32[128,512]{1,0:T(8,128)} async-done(((f32[2048,512]{1,0:T(8,128)}), f32[128,512]{1,0:T(8,128)}) %reduce-scatter.3.cloned.1.call-update) | async-done | bytes 262160 | tf_op jit(solution)/shard_map/reduce_scatter | solution.py:105
  249.2 1.6 convolution_bitcast_fusion.1
  250.8 1.5 pad_maximum_fusion
  252.4 0.9 copy-done
  253.4 0.8 pad_maximum_fusion.1
  254.2 150.9 %all-reduce.2.cloned.1.call-done = f32[2,512,512]{2,1,0:T(8,128)} async-done(((f32[2,512,512]{2,1,0:T(8,128)}), f32[2,512,512]{2,1,0:T(8,128)}) %all-reduce.2.cloned.1.call-update) | async-done | bytes 2097168 | tf_op jit(solution)/shard_map/psum | solution.py:115
  405.1 3.1 neg.3
  (34 shorter events, 1.0 us)
Async XLA Ops:
  14.2 37.8 %all-to-all-start.1 = ((bf16[16,128,512]{2,1,0:T(8,128)(2,1)}), bf16[16,128,512]{2,1,0:T(8,128)(2,1)S(1)}, u32[]{:S(2)}, u32[]{:S(2)}) async-start(bf16[16,128,512]{2,1,0:T(8,128)(2,1)} %copy.41), calls=%async_computation.2 | async-start | bytes 4194304 | tf_op jit(solution)/shard_map/all_to_all | solution.py:82
  23.5 180.2 %reduce-scatter.5.cloned.1.call-start = ((), (), s32[]{:S(2)}) async-start(), calls=%async_computation.7 | async-start | bytes 4456448 | tf_op jit(solution)/shard_map/reduce_scatter | solution.py:105
  70.7 35.6 %all-to-all-start = ((bf16[16,128,512]{2,1,0:T(8,128)(2,1)}), bf16[16,128,512]{2,1,0:T(8,128)(2,1)S(1)}, u32[]{:S(2)}, u32[]{:S(2)}) async-start(bf16[16,128,512]{2,1,0:T(8,128)(2,1)} %copy.37), calls=%async_computation | async-start | bytes 4194304 | tf_op jit(solution)/shard_map/all_to_all | solution.py:82
  77.8 171.4 %reduce-scatter.3.cloned.1.call-start = ((), (), s32[]{:S(2)}) async-start(), calls=%async_computation.6 | async-start | bytes 4456448 | tf_op jit(solution)/shard_map/reduce_scatter | solution.py:105
  123.7 42.0 %all-to-all-start.3 = ((bf16[16,128,512]{2,1,0:T(8,128)(2,1)}), bf16[16,128,512]{2,1,0:T(8,128)(2,1)S(1)}, u32[]{:S(2)}, u32[]{:S(2)}) async-start(bf16[16,128,512]{2,1,0:T(8,128)(2,1)} %copy.47), calls=%async_computation.5 | async-start | bytes 4194304 | tf_op jit(solution)/shard_map/all_to_all | solution.py:17
  165.7 36.2 %all-to-all-start.2 = ((bf16[16,128,512]{2,1,0:T(8,128)(2,1)}), bf16[16,128,512]{2,1,0:T(8,128)(2,1)}, u32[]{:S(2)}, u32[]{:S(2)}) async-start(bf16[16,128,512]{2,1,0:T(8,128)(2,1)} %copy.45), calls=%async_computation.4 | async-start | bytes 4194304 | tf_op jit(solution)/shard_map/all_to_all | solution.py:17
  173.3 231.9 %all-reduce.2.cloned.1.call-start = ((), (), s32[]{:S(2)}) async-start(), calls=%async_computation.8 | async-start | bytes 4194304 | tf_op jit(solution)/shard_map/psum | solution.py:115
  252.3 0.9 copy-start
  252.3 1.0 copy-start.1
Sparse Core Ops, SparseCore 0:
  66.1 95.6 reduce-scatter.4
  166.4 82.7 reduce-scatter.2
  254.6 150.4 all-reduce.1
where the time goes:
time: 416 us; the launch traced here: 415 us
  waiting for transfers between devices  271 us (65%)
  local copies, waits for them, and re-layouts  39.6 us (10%)
  starting transfers between devices  34.9 us (8%)
  matrix products  29.4 us (7%)
  other arithmetic  25.7 us (6%)
  between operations  13.9 us (3%)
    psum x1, waiting for transfers between devices, local(): diag_total = lax.psum(jnp.stack(diag_terms), ('row', 'col'))  151 us
    all_to_all x2, waiting for transfers between devices, sent_and_summed(): lax.all_to_all(pieces, axis, split_axis=0, concat_axis=0, tiled=True)  56.3 us
    reduce_scatter x2, waiting for transfers between devices, local(): lax.psum_scatter(partial_rows(jnp.int32(0), own_rows * lax.axis_size('col...  43.9 us
    all_to_all x2, waiting for transfers between devices, local(): lax.all_to_all(outgoing, 'col', split_axis=0, concat_axis=0, tiled=True)  20.1 us
    gather x4, local copies, waits for them, and re-layouts, local(): picked = a_blocks[local_row[supernode][chosen_pos]]  18.3 us
    all_to_all x2, starting transfers between devices, sent_and_summed(): lax.all_to_all(pieces, axis, split_axis=0, concat_axis=0, tiled=True)  18 us
    dot_general x2, matrix products, partial_rows(): return jnp.dot(picked, chosen, preferred_element_type=jnp.float32)  17.1 us
    all_to_all x2, starting transfers between devices, local(): lax.all_to_all(outgoing, 'col', split_axis=0, concat_axis=0, tiled=True)  16.4 us
  transfers between devices with their start and end apart: 7, of which 6 were waited for; matrix products, arithmetic and copies ran while one was open for 16% of the time, Pallas kernels for 0%

commit v1 on v0

--- a/solution.py
+++ b/solution.py
@@ -112,7 +112,9 @@
         contrib = exact_product(own_left, mine_sums)
         panel_sums.append(mine_sums)
         diag_terms.append(contrib)
-    diag_total = lax.psum(jnp.stack(diag_terms), ("row", "col"))
+    diag_total = jnp.stack(diag_terms)
+    for name in ("col", "row"):
+        diag_total = lax.psum(diag_total, name)
     return (jnp.stack(panel_sums), -diag_total)
 
 

time: 416 us -> 492 us (1.18)
  waiting for transfers between devices: 271 us -> 346 us
    psum x1 -> x2, waiting for transfers between devices: 151 us -> 225 us  [local(): diag_total = lax.psum(diag_total, name)]
  transfers between devices with their start and end apart: 7 -> 8, of which waited for: 6 -> 7; matrix products, arithmetic and copies ran while one was open for 16% -> 14% of each run, Pallas kernels for 0% -> 0%
where the time goes in v1:
time: 492 us; the launch traced here: 488 us
  waiting for transfers between devices  346 us (70%)
  local copies, waits for them, and re-layouts  38.6 us (8%)
  starting transfers between devices  34.9 us (7%)
  matrix products  29.4 us (6%)
  other arithmetic  25.7 us (5%)
  between operations  14 us (3%)
    psum x2, waiting for transfers between devices, local(): diag_total = lax.psum(diag_total, name)  225 us
    all_to_all x2, waiting for transfers between devices, sent_and_summed(): lax.all_to_all(pieces, axis, split_axis=0, concat_axis=0, tiled=True)  56.3 us
    reduce_scatter x2, waiting for transfers between devices, local(): lax.psum_scatter(partial_rows(jnp.int32(0), own_rows * lax.axis_size('col...  43.9 us
    all_to_all x2, waiting for transfers between devices, local(): lax.all_to_all(outgoing, 'col', split_axis=0, concat_axis=0, tiled=True)  20.1 us
    gather x4, local copies, waits for them, and re-layouts, local(): picked = a_blocks[local_row[supernode][chosen_pos]]  18.3 us
    all_to_all x2, starting transfers between devices, sent_and_summed(): lax.all_to_all(pieces, axis, split_axis=0, concat_axis=0, tiled=True)  17.9 us
    dot_general x2, matrix products, partial_rows(): return jnp.dot(picked, chosen, preferred_element_type=jnp.float32)  17.1 us
    all_to_all x2, starting transfers between devices, local(): lax.all_to_all(outgoing, 'col', split_axis=0, concat_axis=0, tiled=True)  16.4 us
  transfers between devices with their start and end apart: 8, of which 7 were waited for; matrix products, arithmetic and copies ran while one was open for 14% of the time, Pallas kernels for 0%

profile of v1, /device:TPU:1, one launch (start us, length us, event | category | flops | bytes accessed | tf_op | source)
XLA Modules:
  0.0 488.2 jit_solution(4170121816032635111)
XLA Ops:
  7.2 0.9 select_reduce_fusion
  8.1 1.3 fusion.60
  9.4 0.6 gather_fusion.8
  10.2 0.6 gather_fusion.9
  10.9 0.9 convolution_convert_fusion.2
  11.7 2.5 copy.41
  14.2 9.3 %all-to-all-start.1 = ((bf16[16,128,512]{2,1,0:T(8,128)(2,1)}), bf16[16,128,512]{2,1,0:T(8,128)(2,1)S(1)}, u32[]{:S(2)}, u32[]{:S(2)}) async-start(bf16[16,128,512]{2,1,0:T(8,128)(2,1)} %copy.41), calls=%async_computation.2 | async-start | bytes 4194304 | tf_op jit(solution)/shard_map/all_to_all | solution.py:82
  23.6 2.0 sort.32
  25.6 0.7 gather_fusion.6
  26.3 0.7 gather_fusion.5
  27.0 8.2 %gather_fusion.7 = bf16[16,128,1664]{2,1,0:T(8,128)(2,1)} fusion(bf16[26,128,1664]{2,1,0:T(8,128)(2,1)} %bitcast.73, s32[1024]{0:T(1024)S(1)} %pad_clamp_fusion), kind=kCustom, calls=%fused_computation.7 | custom fusion | bytes 13631552 | tf_op jit(solution)/shard_map/gather | solution.py:63
  35.2 6.4 %broadcast_select_fusion = bf16[16,128,1664]{2,1,0:T(8,128)(2,1)} fusion(bf16[16,128,1664]{2,1,0:T(8,128)(2,1)} %gather_fusion.7, pred[16]{0:T(512)(128)(4,1)S(1)} %gather_fusion.5), kind=kLoop, calls=%fused_computation.10 | loop fusion | flops 3407872 | bytes 13631504 | tf_op jit(solution)/shard_map/jit(_where)/select_n | solution.py:64
  41.6 10.4 %all-to-all-done.1 = bf16[16,128,512]{2,1,0:T(8,128)(2,1)S(1)} async-done(((bf16[16,128,512]{2,1,0:T(8,128)(2,1)}), bf16[16,128,512]{2,1,0:T(8,128)(2,1)S(1)}, u32[]{:S(2)}, u32[]{:S(2)}) %all-to-all-start.1) | async-done | bytes 2097184 | tf_op jit(solution)/shard_map/all_to_all | solution.py:82
  52.0 2.8 fusion.7
  54.8 2.6 copy.43
  57.4 8.6 %fusion.64 = f32[2048,512]{1,0:T(8,128)} fusion(bf16[2048,1664]{1,0:T(8,128)(2,1)} %bitcast.76, bf16[1664,512]{1,0:T(8,128)(2,1)S(1)} %bitcast.81), kind=kOutput, calls=%fused_computation.117 | convolution fusion | flops 3489660928 | bytes 12713984 | tf_op jit(solution)/shard_map/dot_general | solution.py:103
  66.0 0.6 gather_fusion.3
  66.7 0.6 gather_fusion.4
  67.3 0.9 convolution_convert_fusion.3
  68.2 2.5 copy.37
  70.7 7.1 %all-to-all-start = ((bf16[16,128,512]{2,1,0:T(8,128)(2,1)}), bf16[16,128,512]{2,1,0:T(8,128)(2,1)S(1)}, u32[]{:S(2)}, u32[]{:S(2)}) async-start(bf16[16,128,512]{2,1,0:T(8,128)(2,1)} %copy.37), calls=%async_computation | async-start | bytes 4194304 | tf_op jit(solution)/shard_map/all_to_all | solution.py:82
  78.0 2.0 sort.31
  80.1 0.7 gather_fusion.1
  80.8 8.8 %gather_fusion.2 = bf16[16,128,1664]{2,1,0:T(8,128)(2,1)} fusion(bf16[26,128,1664]{2,1,0:T(8,128)(2,1)} %bitcast.74, s32[1024]{0:T(1024)S(1)} %pad_clamp_fusion.3), kind=kCustom, calls=%fused_computation.2 | custom fusion | bytes 13631552 | tf_op jit(solution)/shard_map/gather | solution.py:63
  89.5 0.7 gather_fusion
  90.2 6.4 %broadcast_select_fusion.1 = bf16[16,128,1664]{2,1,0:T(8,128)(2,1)} fusion(bf16[16,128,1664]{2,1,0:T(8,128)(2,1)} %gather_fusion.2, pred[16]{0:T(512)(128)(4,1)S(1)} %gather_fusion), kind=kLoop, calls=%fused_computation.11 | loop fusion | flops 3407872 | bytes 13631504 | tf_op jit(solution)/shard_map/jit(_where)/select_n | solution.py:64
  96.6 9.7 %all-to-all-done = bf16[16,128,512]{2,1,0:T(8,128)(2,1)S(1)} async-done(((bf16[16,128,512]{2,1,0:T(8,128)(2,1)}), bf16[16,128,512]{2,1,0:T(8,128)(2,1)S(1)}, u32[]{:S(2)}, u32[]{:S(2)}) %all-to-all-start) | async-done | bytes 2097184 | tf_op jit(solution)/shard_map/all_to_all | solution.py:82
  106.3 2.8 fusion.4
  109.1 2.6 copy.39
  111.7 8.5 %fusion.63 = f32[2048,512]{1,0:T(8,128)} fusion(bf16[2048,1664]{1,0:T(8,128)(2,1)} %bitcast.75, bf16[1664,512]{1,0:T(8,128)(2,1)S(1)} %bitcast.82), kind=kOutput, calls=%fused_computation.116 | convolution fusion | flops 3489660928 | bytes 12713984 | tf_op jit(solution)/shard_map/dot_general | solution.py:103
  120.3 0.9 convolution_convert_fusion
  121.2 2.5 copy.47
  123.7 10.4 %all-to-all-start.3 = ((bf16[16,128,512]{2,1,0:T(8,128)(2,1)}), bf16[16,128,512]{2,1,0:T(8,128)(2,1)S(1)}, u32[]{:S(2)}, u32[]{:S(2)}) async-start(bf16[16,128,512]{2,1,0:T(8,128)(2,1)} %copy.47), calls=%async_computation.5 | async-start | bytes 4194304 | tf_op jit(solution)/shard_map/all_to_all | solution.py:17
  134.0 0.9 convolution_convert_fusion.1
  134.9 2.5 copy.45
  137.4 28.3 %all-to-all-done.3 = bf16[16,128,512]{2,1,0:T(8,128)(2,1)S(1)} async-done(((bf16[16,128,512]{2,1,0:T(8,128)(2,1)}), bf16[16,128,512]{2,1,0:T(8,128)(2,1)S(1)}, u32[]{:S(2)}, u32[]{:S(2)}) %all-to-all-start.3) | async-done | bytes 2097184 | tf_op jit(solution)/shard_map/all_to_all | solution.py:17
  165.7 7.5 %all-to-all-start.2 = ((bf16[16,128,512]{2,1,0:T(8,128)(2,1)}), bf16[16,128,512]{2,1,0:T(8,128)(2,1)}, u32[]{:S(2)}, u32[]{:S(2)}) async-start(bf16[16,128,512]{2,1,0:T(8,128)(2,1)} %copy.45), calls=%async_computation.4 | async-start | bytes 4194304 | tf_op jit(solution)/shard_map/all_to_all | solution.py:17
  173.5 0.3 reduce_sum.55
  173.8 28.0 %all-to-all-done.2 = bf16[16,128,512]{2,1,0:T(8,128)(2,1)} async-done(((bf16[16,128,512]{2,1,0:T(8,128)(2,1)}), bf16[16,128,512]{2,1,0:T(8,128)(2,1)}, u32[]{:S(2)}, u32[]{:S(2)}) %all-to-all-start.2) | async-done | bytes 2097184 | tf_op jit(solution)/shard_map/all_to_all | solution.py:17
  201.8 1.9 reduce_sum.54
  203.7 1.6 convolution_bitcast_fusion
  205.3 43.8 %reduce-scatter.3.cloned.1.call-done = f32[128,512]{1,0:T(8,128)} async-done(((f32[2048,512]{1,0:T(8,128)}), f32[128,512]{1,0:T(8,128)}) %reduce-scatter.3.cloned.1.call-update) | async-done | bytes 262160 | tf_op jit(solution)/shard_map/reduce_scatter | solution.py:105
  249.2 1.6 convolution_bitcast_fusion.1
  250.7 1.5 pad_maximum_fusion
  252.4 144.2 %all-reduce.3.cloned.1.call-done = f32[2,512,512]{2,1,0:T(8,128)} async-done(((f32[2,512,512]{2,1,0:T(8,128)}), f32[2,512,512]{2,1,0:T(8,128)}) %all-reduce.3.cloned.1.call-update) | async-done | bytes 2097168 | tf_op jit(solution)/shard_map/psum | solution.py:117
  396.6 0.8 pad_maximum_fusion.1
  397.4 81.1 %all-reduce.5.cloned.1.call-done = f32[2,512,512]{2,1,0:T(8,128)} async-done(((f32[2,512,512]{2,1,0:T(8,128)}), f32[2,512,512]{2,1,0:T(8,128)}) %all-reduce.5.cloned.1.call-update) | async-done | bytes 2097168 | tf_op jit(solution)/shard_map/psum | solution.py:117
  478.5 3.1 neg.3
  (37 shorter events, 1.0 us)
Async XLA Ops:
  14.2 37.8 %all-to-all-start.1 = ((bf16[16,128,512]{2,1,0:T(8,128)(2,1)}), bf16[16,128,512]{2,1,0:T(8,128)(2,1)S(1)}, u32[]{:S(2)}, u32[]{:S(2)}) async-start(bf16[16,128,512]{2,1,0:T(8,128)(2,1)} %copy.41), calls=%async_computation.2 | async-start | bytes 4194304 | tf_op jit(solution)/shard_map/all_to_all | solution.py:82
  23.5 180.2 %reduce-scatter.5.cloned.1.call-start = ((), (), s32[]{:S(2)}) async-start(), calls=%async_computation.7 | async-start | bytes 4456448 | tf_op jit(solution)/shard_map/reduce_scatter | solution.py:105
  70.7 35.6 %all-to-all-start = ((bf16[16,128,512]{2,1,0:T(8,128)(2,1)}), bf16[16,128,512]{2,1,0:T(8,128)(2,1)S(1)}, u32[]{:S(2)}, u32[]{:S(2)}) async-start(bf16[16,128,512]{2,1,0:T(8,128)(2,1)} %copy.37), calls=%async_computation | async-start | bytes 4194304 | tf_op jit(solution)/shard_map/all_to_all | solution.py:82
  77.8 171.4 %reduce-scatter.3.cloned.1.call-start = ((), (), s32[]{:S(2)}) async-start(), calls=%async_computation.6 | async-start | bytes 4456448 | tf_op jit(solution)/shard_map/reduce_scatter | solution.py:105
  123.7 42.0 %all-to-all-start.3 = ((bf16[16,128,512]{2,1,0:T(8,128)(2,1)}), bf16[16,128,512]{2,1,0:T(8,128)(2,1)S(1)}, u32[]{:S(2)}, u32[]{:S(2)}) async-start(bf16[16,128,512]{2,1,0:T(8,128)(2,1)} %copy.47), calls=%async_computation.5 | async-start | bytes 4194304 | tf_op jit(solution)/shard_map/all_to_all | solution.py:17
  165.7 36.1 %all-to-all-start.2 = ((bf16[16,128,512]{2,1,0:T(8,128)(2,1)}), bf16[16,128,512]{2,1,0:T(8,128)(2,1)}, u32[]{:S(2)}, u32[]{:S(2)}) async-start(bf16[16,128,512]{2,1,0:T(8,128)(2,1)} %copy.45), calls=%async_computation.4 | async-start | bytes 4194304 | tf_op jit(solution)/shard_map/all_to_all | solution.py:17
  173.2 223.3 %all-reduce.3.cloned.1.call-start = ((), (), s32[]{:S(2)}) async-start(), calls=%async_computation.8 | async-start | bytes 4194304 | tf_op jit(solution)/shard_map/psum | solution.py:117
  252.3 144.3 %copy-start = (f32[128,512]{1,0:T(8,128)S(1)}, f32[128,512]{1,0:T(8,128)}, u32[]{:S(2)}) copy-start(f32[128,512]{1,0:T(8,128)} %reduce-scatter.5.cloned.1.call-done) | copy-start | bytes 786436
  252.3 144.3 %copy-start.1 = (f32[128,512]{1,0:T(8,128)S(1)}, f32[128,512]{1,0:T(8,128)}, u32[]{:S(2)}) copy-start(f32[128,512]{1,0:T(8,128)} %reduce-scatter.3.cloned.1.call-done) | copy-start | bytes 786436
  252.3 226.2 %all-reduce.5.cloned.1.call-start = ((), (), s32[]{:S(2)}) async-start(), calls=%async_computation.9 | async-start | bytes 4194304 | tf_op jit(solution)/shard_map/psum | solution.py:117
Sparse Core Ops, SparseCore 0:
  66.1 95.5 reduce-scatter.4
  166.3 82.8 reduce-scatter.2
  252.4 144.0 all-reduce.2
  398.9 79.5 all-reduce.4
